TPU v7x, 1024 devices: a whole 4x4x32 slice. The times are simulated.
1024 devices in a mesh: dp: 64 (over z, x_hi), tensor: 16 (over x_lo, y, core).
Axes of the slice: x: 4 (x_hi: 2, x_lo: 2; x = x_hi * 2 + x_lo), y: 4, z: 32, core: 2. Of those that a mesh axis runs over, the one named last changes fastest.
Arguments:
- activations: bfloat16 [384, 8192], P('dp', 'tensor'), may hold values from -6 to 6
- cotangent: bfloat16 [384, 8192], P('dp', 'tensor'), may hold values from -6 to 6
- w_gate: bfloat16 [28672, 8192], P('dp', 'tensor'), may hold values from -0.0625 to 0.0625
- w_up: bfloat16 [28672, 8192], P('dp', 'tensor'), may hold values from -0.0625 to 0.0625
- w_down: bfloat16 [28672, 8192], P('dp', 'tensor'), may hold values from -0.03125 to 0.03125
Outputs:
- output: bfloat16 [384, 8192], P('dp', 'tensor')
- grad_input: bfloat16 [384, 8192], P('dp', 'tensor')
- grad_gate: bfloat16 [28672, 8192], P('dp', 'tensor')
- grad_up: bfloat16 [28672, 8192], P('dp', 'tensor')
- grad_down: bfloat16 [28672, 8192], P('dp', 'tensor')
All inputs are finite; a program needn't handle non-finite values.
Results may differ from a plain program's by a relative error of at most 0.0049.
Values may be sent and summed in bfloat16 or wider, within the bound.
A program may use at most 32 MiB of HBM per device.

v0:
```python
import jax
import jax.numpy as jnp
from jax import lax
from jax.sharding import PartitionSpec as P


def swiglu_pair(gate_sums, up_sums, grad_hidden):
    sigmoid_gate = jax.nn.sigmoid(gate_sums)
    silu_gate = gate_sums * sigmoid_gate
    hidden = (silu_gate * up_sums).astype(jnp.bfloat16)
    d_up = (grad_hidden * silu_gate).astype(jnp.bfloat16)
    d_gate = (
        grad_hidden * up_sums * sigmoid_gate * (1.0 + gate_sums * (1.0 - sigmoid_gate))
    ).astype(jnp.bfloat16)
    return (hidden, d_gate, d_up)


def contract_last(left, right):
    return lax.dot_general(
        left, right, (((1,), (1,)), ((), ())), preferred_element_type=jnp.float32
    )


def contract_first(left, right):
    return lax.dot_general(
        left, right, (((0,), (0,)), ((), ())), preferred_element_type=jnp.float32
    )


def on_device(activations, cotangent, w_gate, w_up, w_down):
    gathered, cot_all = (
        lax.all_gather(activations, "dp", axis=0, tiled=True),
        lax.all_gather(cotangent, "dp", axis=0, tiled=True),
    )
    gate_part = contract_last(gathered, w_gate)
    up_part = contract_last(gathered, w_up)
    grad_part = contract_last(cot_all, w_down)
    gate_sums, up_sums, grad_hidden = (
        lax.psum_scatter(gate_part, "tensor", scatter_dimension=0, tiled=True),
        lax.psum_scatter(up_part, "tensor", scatter_dimension=0, tiled=True),
        lax.psum_scatter(grad_part, "tensor", scatter_dimension=0, tiled=True),
    )
    hidden, d_gate, d_up = swiglu_pair(gate_sums, up_sums, grad_hidden)
    hidden_all, d_gate_all, d_up_all = (
        lax.all_gather(hidden, "tensor", axis=0, tiled=True),
        lax.all_gather(d_gate, "tensor", axis=0, tiled=True),
        lax.all_gather(d_up, "tensor", axis=0, tiled=True),
    )
    grad_gate = contract_first(d_gate_all, gathered).astype(jnp.bfloat16)
    grad_up = contract_first(d_up_all, gathered).astype(jnp.bfloat16)
    grad_down = contract_first(hidden_all, cot_all).astype(jnp.bfloat16)
    forward_term = jnp.dot(hidden_all, w_down, preferred_element_type=jnp.float32)
    backward_term = jnp.dot(d_gate_all, w_gate, preferred_element_type=jnp.float32) + jnp.dot(
        d_up_all, w_up, preferred_element_type=jnp.float32
    )
    summed = lax.psum_scatter(
        jnp.concatenate([forward_term, backward_term], axis=1),
        "dp",
        scatter_dimension=0,
        tiled=True,
    )
    feature_count = activations.shape[1]
    output = summed[:, :feature_count].astype(jnp.bfloat16)
    grad_input = summed[:, feature_count:].astype(jnp.bfloat16)
    return (output, grad_input, grad_gate, grad_up, grad_down)


def solution(mesh):
    return jax.shard_map(
        on_device,
        mesh=mesh,
        in_specs=(
            P("dp", "tensor"),
            P("dp", "tensor"),
            P("dp", "tensor"),
            P("dp", "tensor"),
            P("dp", "tensor"),
        ),
        out_specs=(
            P("dp", "tensor"),
            P("dp", "tensor"),
            P("dp", "tensor"),
            P("dp", "tensor"),
            P("dp", "tensor"),
        ),
        check_vma=False,
    )
```

profile of v0, /device:TPU:6, one launch (start us, length us, event | category | flops | bytes accessed | tf_op | source)
XLA Modules:
  0.0 767.3 jit_solution(11619685725897901502)
XLA Ops:
  7.2 158.8 %all-gather.1 = bf16[64,6,512]{2,1,0:T(8,128)(2,1)S(1)} all-gather(bf16[1,6,512]{2,1,0:T(8,128)(2,1)} %bitcast.23), channel_id=1, replica_groups=mesh['dp'=64,'tensor'=16] {'dp'}, dimensions={0}, use_global_device_ids=true | all-gather | bytes 399360 | tf_op jit(solution)/shard_map/all_gather | solution.py:33
  166.1 1.3 fusion.7
  167.5 147.4 %all-gather = bf16[64,6,512]{2,1,0:T(8,128)(2,1)S(1)} all-gather(bf16[1,6,512]{2,1,0:T(8,128)(2,1)S(1)} %bitcast.24), channel_id=1, replica_groups=mesh['dp'=64,'tensor'=16] {'dp'}, dimensions={0}, use_global_device_ids=true | all-gather | bytes 399360 | tf_op jit(solution)/shard_map/all_gather | solution.py:32
  315.0 1.3 fusion.5
  316.4 1.3 fusion.4
  317.8 67.9 %reduce-scatter.8.cloned.1.call-done = f32[24,448]{1,0:T(8,128)} async-done(((f32[384,448]{1,0:T(8,128)}), f32[24,448]{1,0:T(8,128)}) %reduce-scatter.8.cloned.1.call-update) | async-done | bytes 43024 | tf_op jit(solution)/shard_map/reduce_scatter | solution.py:40
  385.7 81.0 %reduce-scatter.6.cloned.1.call-done = f32[24,448]{1,0:T(8,128)} async-done(((f32[384,448]{1,0:T(8,128)}), f32[24,448]{1,0:T(8,128)}) %reduce-scatter.6.cloned.1.call-update) | async-done | bytes 43024 | tf_op jit(solution)/shard_map/reduce_scatter | solution.py:39
  467.6 17.0 %all_gather.16 = bf16[384,448]{1,0:T(8,128)(2,1)S(1)} all-gather(bf16[24,448]{1,0:T(8,128)(2,1)S(1)} %get-tuple-element.5), channel_id=1, replica_groups=mesh['dp'=64,'tensor'=16] {'tensor'}, dimensions={0}, use_global_device_ids=true | all-gather | bytes 365568 | tf_op jit(solution)/shard_map/all_gather | solution.py:45
  484.6 19.0 %all_gather.18 = bf16[384,448]{1,0:T(8,128)(2,1)S(1)} all-gather(bf16[24,448]{1,0:T(8,128)(2,1)S(1)} %get-tuple-element.6), channel_id=1, replica_groups=mesh['dp'=64,'tensor'=16] {'tensor'}, dimensions={0}, use_global_device_ids=true | all-gather | bytes 365568 | tf_op jit(solution)/shard_map/all_gather | solution.py:46
  503.5 17.3 %all_gather.19 = bf16[384,448]{1,0:T(8,128)(2,1)S(1)} all-gather(bf16[24,448]{1,0:T(8,128)(2,1)S(1)} %get-tuple-element.7), channel_id=1, replica_groups=mesh['dp'=64,'tensor'=16] {'tensor'}, dimensions={0}, use_global_device_ids=true | all-gather | bytes 365568 | tf_op jit(solution)/shard_map/all_gather | solution.py:47
  521.2 1.4 fusion.8
  523.2 160.8 %fusion = f32[8,1024]{1,0:T(8,128)S(1)} fusion(f32[384,1024]{1,0:T(8,128)S(1)} %pad_maximum_fusion), kind=kCustom, calls=%all-reduce-scatter | all-reduce-scatter fusion | flops 524289 | bytes 1609728
  684.0 10.3 %collective-permute-start.15 = (bf16[6,1024]{1,0:T(8,128)(2,1)S(1)}, bf16[6,1024]{1,0:T(8,128)(2,1)S(1)}, u32[]{:S(2)}, u32[]{:S(2)}) collective-permute-start(bf16[6,1024]{1,0:T(8,128)(2,1)S(1)} %slice.12), channel_id=1, source_target_pairs={{0,256},{16,272},{32,288},{48,304},{64,320},{80,336},{96,352},{112... | collective-permute-start | bytes 36872
  694.3 1.3 dynamic-slice.4
  696.3 1.3 collective-permute-start.1
  697.6 7.0 collective-permute-start.2
  704.6 5.3 collective-permute-start.3
  709.9 6.3 collective-permute-start.4
  716.2 4.8 collective-permute-start.5
  721.0 2.2 convolution_convert_fusion
  723.2 5.7 collective-permute-start.6
  728.9 1.9 collective-permute-start.7
  730.8 4.8 collective-permute-start.8
  735.6 1.9 collective-permute-start.9
  737.6 2.2 collective-permute-start.10
  741.0 1.5 collective-permute-start.11
  742.5 3.8 collective-permute-start.12
  746.3 1.3 collective-permute-start.13
  747.6 3.4 collective-permute-start.14
  751.1 3.3 collective-permute-start
  755.6 2.6 collective-permute-done
  758.2 1.9 concatenate.4
  (50 shorter events, 5.3 us)
Async XLA Ops:
  7.2 159.0 %copy-start = (bf16[448,512]{1,0:T(8,128)(2,1)S(1)}, bf16[448,512]{1,0:T(8,128)(2,1)}, u32[]{:S(2)}) copy-start(bf16[448,512]{1,0:T(8,128)(2,1)} %param.9) | copy-start | bytes 1376260
  7.2 310.6 %reduce-scatter.10.cloned.1.call-start = ((), (), s32[]{:S(2)}) async-start(), calls=%async_computation.5 | async-start | bytes 835584 | tf_op jit(solution)/shard_map/reduce_scatter | solution.py:41
  166.0 1.5 copy-start.7
  166.1 148.9 %copy-start.4 = (bf16[448,512]{1,0:T(8,128)(2,1)S(1)}, bf16[448,512]{1,0:T(8,128)(2,1)}, u32[]{:S(2)}) copy-start(bf16[448,512]{1,0:T(8,128)(2,1)} %param.8) | copy-start | bytes 1376260
  167.5 218.3 %reduce-scatter.8.cloned.1.call-start = ((), (), s32[]{:S(2)}) async-start(), calls=%async_computation.4 | async-start | bytes 835584 | tf_op jit(solution)/shard_map/reduce_scatter | solution.py:40
  314.9 1.5 copy-start.6
  316.4 150.3 %reduce-scatter.6.cloned.1.call-start = ((), (), s32[]{:S(2)}) async-start(), calls=%async_computation.3 | async-start | bytes 835584 | tf_op jit(solution)/shard_map/reduce_scatter | solution.py:39
  484.6 38.0 %copy-start.3 = (bf16[384,448]{1,0:T(8,128)(2,1)}, bf16[384,448]{1,0:T(8,128)(2,1)S(1)}, u32[]{:S(2)}) copy-start(bf16[384,448]{1,0:T(8,128)(2,1)S(1)} %all_gather.16) | copy-start | bytes 1032196
  503.5 19.1 %copy-start.1 = (bf16[384,448]{1,0:T(8,128)(2,1)}, bf16[384,448]{1,0:T(8,128)(2,1)S(1)}, u32[]{:S(2)}) copy-start(bf16[384,448]{1,0:T(8,128)(2,1)S(1)} %all_gather.18) | copy-start | bytes 1032196
  520.9 1.8 copy-start.5
  684.0 70.4 %copy-start.2 = (bf16[384,448]{1,0:T(8,128)(2,1)S(1)}, bf16[384,448]{1,0:T(8,128)(2,1)}, u32[]{:S(2)}) copy-start(bf16[384,448]{1,0:T(8,128)(2,1)} %copy-done.1) | copy-start | bytes 1032196
  684.0 32.2 %collective-permute-start.15 = (bf16[6,1024]{1,0:T(8,128)(2,1)S(1)}, bf16[6,1024]{1,0:T(8,128)(2,1)S(1)}, u32[]{:S(2)}, u32[]{:S(2)}) collective-permute-start(bf16[6,1024]{1,0:T(8,128)(2,1)S(1)} %slice.12), channel_id=1, source_target_pairs={{0,256},{16,272},{32,288},{48,304},{64,320},{80,336},{96,352},{112... | collective-permute-start | bytes 36872
  696.3 26.9 %collective-permute-start.1 = (bf16[8,1024]{1,0:T(8,128)(2,1)S(1)}, bf16[8,1024]{1,0:T(8,128)(2,1)S(1)}, u32[]{:S(2)}, u32[]{:S(2)}) collective-permute-start(bf16[8,1024]{1,0:T(8,128)(2,1)S(1)} %convert.36), channel_id=1, source_target_pairs={{0,32},{16,48},{32,64},{48,80},{64,96},{80,112},{96,128},{112,144}... | collective-permute-start | bytes 49160
  697.6 31.3 %collective-permute-start.2 = (bf16[8,1024]{1,0:T(8,128)(2,1)S(1)}, bf16[8,1024]{1,0:T(8,128)(2,1)S(1)}, u32[]{:S(2)}, u32[]{:S(2)}) collective-permute-start(bf16[8,1024]{1,0:T(8,128)(2,1)S(1)} %convert.36), channel_id=1, source_target_pairs={{0,48},{16,64},{32,80},{48,96},{64,112},{80,128},{96,144},{112,160... | collective-permute-start | bytes 49160
  704.6 26.2 %collective-permute-start.3 = (bf16[8,1024]{1,0:T(8,128)(2,1)S(1)}, bf16[8,1024]{1,0:T(8,128)(2,1)S(1)}, u32[]{:S(2)}, u32[]{:S(2)}) collective-permute-start(bf16[8,1024]{1,0:T(8,128)(2,1)S(1)} %convert.36), channel_id=1, source_target_pairs={{0,64},{16,80},{32,96},{48,112},{64,128},{80,144},{96,160},{112,17... | collective-permute-start | bytes 49160
  709.9 25.7 %collective-permute-start.4 = (bf16[8,1024]{1,0:T(8,128)(2,1)S(1)}, bf16[8,1024]{1,0:T(8,128)(2,1)S(1)}, u32[]{:S(2)}, u32[]{:S(2)}) collective-permute-start(bf16[8,1024]{1,0:T(8,128)(2,1)S(1)} %convert.36), channel_id=1, source_target_pairs={{0,80},{16,96},{32,112},{48,128},{64,144},{80,160},{96,176},{112,1... | collective-permute-start | bytes 49160
  716.2 21.3 %collective-permute-start.5 = (bf16[8,1024]{1,0:T(8,128)(2,1)S(1)}, bf16[8,1024]{1,0:T(8,128)(2,1)S(1)}, u32[]{:S(2)}, u32[]{:S(2)}) collective-permute-start(bf16[8,1024]{1,0:T(8,128)(2,1)S(1)} %convert.36), channel_id=1, source_target_pairs={{0,96},{16,112},{32,128},{48,144},{64,160},{80,176},{96,192},{112,... | collective-permute-start | bytes 49160
  723.2 17.8 %collective-permute-start.6 = (bf16[8,1024]{1,0:T(8,128)(2,1)S(1)}, bf16[8,1024]{1,0:T(8,128)(2,1)S(1)}, u32[]{:S(2)}, u32[]{:S(2)}) collective-permute-start(bf16[8,1024]{1,0:T(8,128)(2,1)S(1)} %convert.36), channel_id=1, source_target_pairs={{0,112},{16,128},{32,144},{48,160},{64,176},{80,192},{96,208},{112... | collective-permute-start | bytes 49160
  728.9 13.6 %collective-permute-start.7 = (bf16[8,1024]{1,0:T(8,128)(2,1)S(1)}, bf16[8,1024]{1,0:T(8,128)(2,1)S(1)}, u32[]{:S(2)}, u32[]{:S(2)}) collective-permute-start(bf16[8,1024]{1,0:T(8,128)(2,1)S(1)} %convert.36), channel_id=1, source_target_pairs={{0,128},{16,144},{32,160},{48,176},{64,192},{80,208},{96,224},{112... | collective-permute-start | bytes 49160
  730.8 15.5 %collective-permute-start.8 = (bf16[8,1024]{1,0:T(8,128)(2,1)S(1)}, bf16[8,1024]{1,0:T(8,128)(2,1)S(1)}, u32[]{:S(2)}, u32[]{:S(2)}) collective-permute-start(bf16[8,1024]{1,0:T(8,128)(2,1)S(1)} %convert.36), channel_id=1, source_target_pairs={{0,144},{16,160},{32,176},{48,192},{64,208},{80,224},{96,240},{112... | collective-permute-start | bytes 49160
  735.6 12.0 %collective-permute-start.9 = (bf16[8,1024]{1,0:T(8,128)(2,1)S(1)}, bf16[8,1024]{1,0:T(8,128)(2,1)S(1)}, u32[]{:S(2)}, u32[]{:S(2)}) collective-permute-start(bf16[8,1024]{1,0:T(8,128)(2,1)S(1)} %convert.36), channel_id=1, source_target_pairs={{0,160},{16,176},{32,192},{48,208},{64,224},{80,240},{96,256},{112... | collective-permute-start | bytes 49160
  737.6 13.5 %collective-permute-start.10 = (bf16[8,1024]{1,0:T(8,128)(2,1)S(1)}, bf16[8,1024]{1,0:T(8,128)(2,1)S(1)}, u32[]{:S(2)}, u32[]{:S(2)}) collective-permute-start(bf16[8,1024]{1,0:T(8,128)(2,1)S(1)} %convert.36), channel_id=1, source_target_pairs={{0,176},{16,192},{32,208},{48,224},{64,240},{80,256},{96,272},{112... | collective-permute-start | bytes 49160
  741.0 14.6 %collective-permute-start.11 = (bf16[8,1024]{1,0:T(8,128)(2,1)S(1)}, bf16[8,1024]{1,0:T(8,128)(2,1)S(1)}, u32[]{:S(2)}, u32[]{:S(2)}) collective-permute-start(bf16[8,1024]{1,0:T(8,128)(2,1)S(1)} %convert.36), channel_id=1, source_target_pairs={{0,192},{16,208},{32,224},{48,240},{64,256},{80,272},{96,288},{112... | collective-permute-start | bytes 49160
  742.5 13.1 %collective-permute-start.12 = (bf16[8,1024]{1,0:T(8,128)(2,1)S(1)}, bf16[8,1024]{1,0:T(8,128)(2,1)S(1)}, u32[]{:S(2)}, u32[]{:S(2)}) collective-permute-start(bf16[8,1024]{1,0:T(8,128)(2,1)S(1)} %convert.36), channel_id=1, source_target_pairs={{0,208},{16,224},{32,240},{48,256},{64,272},{80,288},{96,304},{112... | collective-permute-start | bytes 49160
  746.3 9.3 %collective-permute-start.13 = (bf16[8,1024]{1,0:T(8,128)(2,1)S(1)}, bf16[8,1024]{1,0:T(8,128)(2,1)S(1)}, u32[]{:S(2)}, u32[]{:S(2)}) collective-permute-start(bf16[8,1024]{1,0:T(8,128)(2,1)S(1)} %convert.36), channel_id=1, source_target_pairs={{0,224},{16,240},{32,256},{48,272},{64,288},{80,304},{96,320},{112... | collective-permute-start | bytes 49160
  747.6 8.0 %collective-permute-start.14 = (bf16[8,1024]{1,0:T(8,128)(2,1)S(1)}, bf16[8,1024]{1,0:T(8,128)(2,1)S(1)}, u32[]{:S(2)}, u32[]{:S(2)}) collective-permute-start(bf16[8,1024]{1,0:T(8,128)(2,1)S(1)} %convert.36), channel_id=1, source_target_pairs={{0,240},{16,256},{32,272},{48,288},{64,304},{80,320},{96,336},{112... | collective-permute-start | bytes 49160
  751.1 7.1 collective-permute-start
Sparse Core Ops, SparseCore 0:
  167.6 71.7 reduce-scatter.9
  316.5 69.1 reduce-scatter.7
  389.1 77.5 reduce-scatter.5
where the time goes:
time: 768 us; the launch traced here: 767 us
  blocking collectives  520 us (68%)
  waiting for transfers between devices  152 us (20%)
  starting transfers between devices  65 us (8%)
  between operations  14.8 us (2%)
  matrix products  10.5 us (1%)
    unnamed x1, blocking collectives  161 us
    all_gather x1, blocking collectives, on_device(): lax.all_gather(cotangent, 'dp', axis=0, tiled=True)  159 us
    all_gather x1, blocking collectives, on_device(): lax.all_gather(activations, 'dp', axis=0, tiled=True)  147 us
    reduce_scatter x1, waiting for transfers between devices, on_device(): lax.psum_scatter(gate_part, 'tensor', scatter_dimension=0, tiled=True)  81 us
    reduce_scatter x1, waiting for transfers between devices, on_device(): lax.psum_scatter(up_part, 'tensor', scatter_dimension=0, tiled=True)  67.9 us
    unnamed x16, starting transfers between devices  64.9 us
    all_gather x1, blocking collectives, on_device(): lax.all_gather(d_gate, 'tensor', axis=0, tiled=True)  19 us
    all_gather x1, blocking collectives, on_device(): lax.all_gather(d_up, 'tensor', axis=0, tiled=True)  17.3 us
  transfers between devices with their start and end apart: 19, of which 3 were waited for; matrix products, arithmetic and copies ran while one was open for 1% of the time, Pallas kernels for 0%

commit v1 on v0

v1 whole, which is shorter than its diff:
```python
import functools

import jax
import jax.numpy as jnp
import numpy as np
from jax import lax
from jax.experimental import pallas as pl
from jax.experimental.pallas import tpu as pltpu
from jax.sharding import PartitionSpec as P

MESH = pl.DeviceIdType.MESH
F32 = jnp.float32
BF16 = jnp.bfloat16

NEAR = (0, 1, -1, 2, -2, 3, -3, 4)
FAR = (0, 8, -8, 16)
TOK = 6
QUARTERS = 4
ROWS = 2 * TOK * QUARTERS
GROUP = TOK * len(NEAR)
N_COPIES = 160


def selections():
    fold = np.zeros((QUARTERS, ROWS, 16), np.float32)
    unfold = np.zeros((QUARTERS, 2 * GROUP, 8 * ROWS), np.float32)
    last = np.zeros((QUARTERS, 16, ROWS), np.float32)
    for q in range(QUARTERS):
        for a in range(2):
            for t in range(TOK):
                row = q * 2 * TOK + a * TOK + t
                fold[q, row, a * 8 + t] = 1
                last[q, a * 8 + t, row] = 1
                for w in range(8):
                    unfold[q, a * GROUP + w * TOK + t, w * ROWS + row] = 1
    back = np.transpose(unfold, (0, 2, 1))
    return [jnp.asarray(v, BF16) for v in (fold, unfold, back, last)]


def dot(a, b):
    return lax.dot_general(a, b, (((1,), (0,)), ((), ())), preferred_element_type=F32)


def dot_t(a, b):
    return lax.dot_general(a, b, (((1,), (1,)), ((), ())), preferred_element_type=F32)


def t_dot(a, b):
    return lax.dot_general(a, b, (((0,), (0,)), ((), ())), preferred_element_type=F32)


def kernel(
    zs, act_ref, cot_ref, wg_hbm, wu_hbm, wd_hbm, fold_ref, unfold_hbm, back_hbm, last_ref,
    out_ref, gin_ref, gg_ref, gu_ref, gd_ref,
    wg, wu, wd, unfold, back, stage16, g_buf, acts, cots,
    pa, pb, ra, rb, qa, qb, a1, b1, sa, sb, a2, b2, ha, hb, hd,
    own_sum, xs, xr_buf, rbuf, rw, rw7a, rw7b, fsend, frecv,
    local_sem, send_sem, recv_sem,
):
    dp, tn = lax.axis_index("dp"), lax.axis_index("tensor")
    z, xh = dp // 2, dp % 2
    xl, y, c = tn // 8, (tn // 2) % 4, tn % 2
    xo, co = 1 - xl, 1 - c

    def z_dev(d):
        return (((z + (d + zs)) % zs) * 2 + xh, tn)

    def t_dev(x_, y_, c_):
        return (dp, (x_ * 4 + y_) * 2 + c_)

    def y_at(d):
        return (y + d) % 4

    x2_dev = (z * 2 + (1 - xh), tn)
    x1_dev = t_dev(xo, y, c)
    c_dev = t_dev(xl, y, co)

    loads = []
    for i, (s, d) in enumerate(
        ((wg_hbm, wg), (wu_hbm, wu), (wd_hbm, wd), (unfold_hbm, unfold), (back_hbm, back))
    ):
        cp = pltpu.make_async_copy(s, d, local_sem.at[i])
        cp.start()
        loads.append(cp)

    barrier = pltpu.get_barrier_semaphore()
    peers = [z_dev(d) for d in (8, -8, 4, -4, 3, -3, 2, -2, 1, -1)]
    peers += [x2_dev, x1_dev, c_dev] + [t_dev(xl, y_at(d), c) for d in (1, 2, 3)]
    for peer in peers:
        pl.semaphore_signal(barrier, inc=1, device_id=peer, device_id_type=MESH)

    sent = []

    def send(src, dst, dev):
        i = len(sent)
        cp = pltpu.make_async_remote_copy(
            src_ref=src, dst_ref=dst, send_sem=send_sem.at[i], recv_sem=recv_sem.at[i],
            device_id=dev, device_id_type=MESH,
        )
        cp.start()
        sent.append(cp)
        return cp

    stage16[...] = jnp.zeros_like(stage16)
    stage16[0:TOK] = act_ref[...].astype(F32)
    stage16[8 : 8 + TOK] = cot_ref[...].astype(F32)
    raw = stage16[...].astype(BF16)
    block = jnp.zeros((ROWS, 128), F32)
    for q in range(QUARTERS):
        block += dot(fold_ref[q], raw[:, q * 128 : (q + 1) * 128])
    g_buf[0, 0, 0] = block.astype(BF16)

    pl.semaphore_wait(barrier, len(peers))

    far = {}
    far[2] = send(g_buf.at[0, 0, 0], g_buf.at[0, 2, 0], z_dev(8))
    far[1] = send(g_buf.at[0, 0, 0], g_buf.at[0, 1, 0], z_dev(-8))
    near = {}

    def spread(f):
        for w in range(1, 7):
            near[f, w] = send(g_buf.at[0, f, 0], g_buf.at[0, f, w], z_dev(-NEAR[w]))
        if f in (0, 1):
            near[f, 7] = send(g_buf.at[0, f, 0], g_buf.at[0, f, 7], z_dev(-4))
        if f in (0, 2):
            near[2 if f == 0 else 3, 7] = send(
                g_buf.at[0, f, 0], g_buf.at[0, 2 if f == 0 else 3, 7], z_dev(4)
            )

    across = {}

    def cross(f):
        for w in range(1, 8):
            near[f, w].wait_recv()
        across[f] = send(g_buf.at[0, f], g_buf.at[1, f], x2_dev)

    def order(x, f):
        blocks = g_buf[x, f].reshape(8 * ROWS, 128)
        for q in range(QUARTERS):
            rows = dot(unfold[q], blocks).astype(BF16)
            lanes = slice(q * 128, (q + 1) * 128)
            acts[x, f, :, lanes] = rows[:GROUP]
            cots[x, f, :, lanes] = rows[GROUP:]

    spread(0)
    far[2].wait_recv()
    far[3] = send(g_buf.at[0, 2, 0], g_buf.at[0, 3, 0], z_dev(8))
    spread(2)
    far[1].wait_recv()
    spread(1)
    for cp in loads:
        cp.wait()
    cross(0)
    order(0, 0)
    far[3].wait_recv()
    spread(3)
    cross(1)
    cross(2)
    order(0, 1)
    order(0, 2)
    across[0].wait_recv()
    order(1, 0)
    cross(3)
    order(0, 3)

    pair = {}

    def partial_sums(x):
        a_rows = acts[x].reshape(4 * GROUP, 512)
        c_rows = cots[x].reshape(4 * GROUP, 512)
        for j, (rows, weight) in enumerate(((a_rows, wg), (a_rows, wu), (c_rows, wd))):
            part = slice(j * GROUP, (j + 1) * GROUP)
            low = dot_t(rows, weight[0:256])
            high = dot_t(rows, weight[256:448])
            for f in range(4):
                r = slice(f * GROUP, (f + 1) * GROUP)
                pa[0, f, x, part] = low[r, 0:128]
                pb[0, x, f, part] = low[r, 128:256]
                pa[1, f, x, part] = high[r, 0:128]
                pb[1, x, f, part, 0:64] = high[r, 128:192]
                pb[1, x, f, part, 64:128] = jnp.zeros((GROUP, 64), F32)
        pair[x, 0] = send(pa.at[co, :, x], ra.at[:, x], c_dev)
        pair[x, 1] = send(pb.at[co, x], rb.at[x], c_dev)

    partial_sums(0)
    for f in (1, 2, 3):
        across[f].wait_recv()
        order(1, f)
    partial_sums(1)

    pair[0, 1].wait_recv()
    pair[1, 1].wait_recv()
    qb[...] = pb[c] + rb[...]
    first_b = send(qb.at[xo], b1, x1_dev)
    pair[0, 0].wait_recv()
    pair[1, 0].wait_recv()
    qa[...] = pa[c] + ra[...]
    first_a = [send(qa.at[y_at(d)], a1.at[d - 1], t_dev(xl, y_at(d), c)) for d in (2, 1, 3)]
    first_b.wait_recv()
    sb[...] = qb[xl] + b1[...]
    second_b = [send(sb.at[y_at(d)], b2.at[d - 1], t_dev(xl, y_at(d), c)) for d in (2, 1, 3)]
    for cp in first_a:
        cp.wait_recv()
    sa[...] = qa[y] + a1[0] + a1[1] + a1[2]
    second_a = send(sa.at[xo], a2, x1_dev)

    def finish(sums):
        gate, up, grad = sums[0:GROUP], sums[GROUP : 2 * GROUP], sums[2 * GROUP : 3 * GROUP]
        s = jax.nn.sigmoid(gate)
        silu = gate * s
        hidden = (silu * up).astype(BF16)
        d_gate = (grad * up * s * (1.0 + gate * (1.0 - s))).astype(BF16)
        d_up = (grad * silu).astype(BF16)
        return jnp.concatenate([hidden, d_gate, d_up], axis=0)

    y_peers = [(d, t_dev(xl, y_at(d), c)) for d in (2, 1, 3)]
    cores = []
    second_a.wait_recv()
    ha[c, y, xl] = finish(sa[xl] + a2[...])
    near_a = send(ha.at[c, y, xl], ha.at[c, y, xl], x1_dev)
    for cp in second_b:
        cp.wait_recv()
    hb[c, xl, y] = finish(sb[y] + b2[0] + b2[1] + b2[2])
    near_b = [send(hb.at[c, xl, y], hb.at[c, xl, y], dev) for d, dev in y_peers]
    near_a.wait_recv()
    wide_a = [send(ha.at[c, y], ha.at[c, y], dev) for d, dev in y_peers]
    cores.append(send(ha.at[c, y], ha.at[c, y], c_dev))
    for cp in near_b:
        cp.wait_recv()
    wide_b = send(hb.at[c, xl], hb.at[c, xl], x1_dev)
    cores.append(send(hb.at[c, xl], hb.at[c, xl], c_dev))
    for (d, dev), cp in zip(y_peers, wide_a):
        cp.wait_recv()
        cores.append(send(ha.at[c, y_at(4 - d)], ha.at[c, y_at(4 - d)], c_dev))
    wide_b.wait_recv()
    cores.append(send(hb.at[c, xo], hb.at[c, xo], c_dev))
    for cp in cores:
        cp.wait_recv()

    for j in range(3):
        part = slice(j * GROUP, (j + 1) * GROUP)
        for half in range(2):
            for x in range(2):
                for f in range(4):
                    hd[j, x, f, :, half * 256 : half * 256 + 128] = ha[half, f, x, part]
                    hd[j, x, f, :, half * 256 + 128 : half * 256 + 256] = hb[half, x, f, part]

    def hidden_sums(x):
        h, dg, du = [hd[j, x].reshape(4 * GROUP, 512)[:, :448] for j in range(3)]
        return dot(h, wd[...]), dot(dg, wg[...]) + dot(du, wu[...])

    f_order = (3, 2, 1, 0)
    fwd, bwd = hidden_sums(1)
    over = {}
    for f in f_order:
        r = slice(f * GROUP, (f + 1) * GROUP)
        xs[f, 0:GROUP] = fwd[r].astype(BF16)
        xs[f, GROUP : 2 * GROUP] = bwd[r].astype(BF16)
        over[f] = send(xs.at[f], xr_buf.at[f], x2_dev)
    fwd, bwd = hidden_sums(0)
    for f in f_order:
        r = slice(f * GROUP, (f + 1) * GROUP)
        own_sum[f, 0:GROUP] = fwd[r]
        own_sum[f, GROUP : 2 * GROUP] = bwd[r]

    step3, step0 = {}, {}
    for f in f_order:
        over[f].wait_recv()
        both = (own_sum[f] + xr_buf[f].astype(F32)).astype(BF16)
        rows = jnp.zeros((8 * ROWS, 128), F32)
        for q in range(QUARTERS):
            rows += dot(back[q], both[:, q * 128 : (q + 1) * 128])
        rows = rows.astype(BF16)
        for w in range(8):
            rbuf[w, f] = rows[w * ROWS : (w + 1) * ROWS]
        if f == 3:
            for w in range(1, 7):
                step3[w] = send(rbuf.at[w, 3], rw.at[w, 3], z_dev(NEAR[w]))
        if f == 2:
            minus4 = send(rbuf.at[7, pl.ds(2, 2)], rw7b, z_dev(-4))
    for w in range(1, 7):
        step0[w] = send(rbuf.at[w, pl.ds(0, 3)], rw.at[w, pl.ds(0, 3)], z_dev(NEAR[w]))
    plus4 = send(rbuf.at[7, pl.ds(0, 2)], rw7a, z_dev(4))

    def near_sum(f):
        total = rbuf[0, f].astype(F32)
        for w in range(1, 7):
            total += rw[w, f].astype(F32)
        return total

    for w in range(1, 7):
        step3[w].wait_recv()
    fsend[0] = near_sum(3).astype(BF16)
    far16 = send(fsend.at[0], frecv.at[0], z_dev(8))

    for w in range(1, 7):
        step0[w].wait_recv()
    minus4.wait_recv()
    plus4.wait_recv()
    fsend[1] = (near_sum(2) + rw7b[1].astype(F32)).astype(BF16)
    back8 = send(fsend.at[1], frecv.at[1], z_dev(-8))

    a_all = acts[...].reshape(8 * GROUP, 512)
    c_all = cots[...].reshape(8 * GROUP, 512)

    def weight_grad(j, rows, ref):
        d = hd[j].reshape(8 * GROUP, 512)
        ref[0:256] = t_dot(d[:, 0:256], rows).astype(BF16)
        ref[256:448] = t_dot(d[:, 256:448], rows).astype(BF16)

    weight_grad(1, a_all, gg_ref)
    weight_grad(2, a_all, gu_ref)
    far16.wait_recv()
    fsend[2] = (near_sum(1) + rw7a[1].astype(F32) + frecv[0].astype(F32)).astype(BF16)
    on8 = send(fsend.at[2], frecv.at[2], z_dev(8))
    weight_grad(0, c_all, gd_ref)

    total = near_sum(0) + rw7a[0].astype(F32) + rw7b[0].astype(F32)
    back8.wait_recv()
    total += frecv[1].astype(F32)
    on8.wait_recv()
    total = (total + frecv[2].astype(F32)).astype(BF16)
    for q in range(QUARTERS):
        stage16[:, q * 128 : (q + 1) * 128] = dot(last_ref[q], total)
    out_ref[...] = stage16[0:TOK].astype(BF16)
    gin_ref[...] = stage16[8 : 8 + TOK].astype(BF16)
    for cp in sent:
        cp.wait_send()


def on_device(zs, activations, cotangent, w_gate, w_up, w_down):
    tokens, features = activations.shape
    hidden = w_gate.shape[0]
    fold, unfold, back, last = selections()
    vmem = pl.BlockSpec(memory_space=pltpu.VMEM)
    anywhere = pl.BlockSpec(memory_space=pl.ANY)
    weight = (hidden, features)
    row3 = 3 * GROUP
    scratch = [
        pltpu.VMEM(weight, BF16), pltpu.VMEM(weight, BF16), pltpu.VMEM(weight, BF16),
        pltpu.VMEM(unfold.shape, BF16), pltpu.VMEM(back.shape, BF16),
        pltpu.VMEM((16, features), F32),
        pltpu.VMEM((2, 4, 8, ROWS, 128), BF16),
        pltpu.VMEM((2, 4, GROUP, features), BF16), pltpu.VMEM((2, 4, GROUP, features), BF16),
        pltpu.VMEM((2, 4, 2, row3, 128), F32), pltpu.VMEM((2, 2, 4, row3, 128), F32),
        pltpu.VMEM((4, 2, row3, 128), F32), pltpu.VMEM((2, 4, row3, 128), F32),
        pltpu.VMEM((4, 2, row3, 128), F32), pltpu.VMEM((2, 4, row3, 128), F32),
        pltpu.VMEM((3, 2, row3, 128), F32), pltpu.VMEM((4, row3, 128), F32),
        pltpu.VMEM((2, row3, 128), F32), pltpu.VMEM((4, row3, 128), F32),
        pltpu.VMEM((row3, 128), F32), pltpu.VMEM((3, row3, 128), F32),
        pltpu.VMEM((2, 4, 2, row3, 128), BF16), pltpu.VMEM((2, 2, 4, row3, 128), BF16),
        pltpu.VMEM((3, 2, 4, GROUP, 512), BF16),
        pltpu.VMEM((4, 2 * GROUP, features), F32),
        pltpu.VMEM((4, 2 * GROUP, features), BF16), pltpu.VMEM((4, 2 * GROUP, features), BF16),
        pltpu.VMEM((8, 4, ROWS, 128), BF16), pltpu.VMEM((8, 4, ROWS, 128), BF16),
        pltpu.VMEM((2, ROWS, 128), BF16), pltpu.VMEM((2, ROWS, 128), BF16),
        pltpu.VMEM((3, ROWS, 128), BF16), pltpu.VMEM((3, ROWS, 128), BF16),
        pltpu.SemaphoreType.DMA((5,)),
        pltpu.SemaphoreType.DMA((N_COPIES,)), pltpu.SemaphoreType.DMA((N_COPIES,)),
    ]
    block = jax.ShapeDtypeStruct((tokens, features), BF16)
    grad = jax.ShapeDtypeStruct(weight, BF16)
    return pl.pallas_call(
        functools.partial(kernel, zs),
        out_shape=(block, block, grad, grad, grad),
        in_specs=[vmem, vmem, anywhere, anywhere, anywhere, vmem, anywhere, anywhere, vmem],
        out_specs=(vmem,) * 5,
        scratch_shapes=scratch,
        compiler_params=pltpu.CompilerParams(
            collective_id=0, has_side_effects=True, vmem_limit_bytes=56 * 2**20
        ),
        cost_estimate=pl.CostEstimate(
            flops=18 * 384 * hidden * features, bytes_accessed=12 * hidden * features,
            transcendentals=0,
        ),
        name="ffn",
    )(activations, cotangent, w_gate, w_up, w_down, fold, unfold, back, last)


def solution(mesh):
    spec = P("dp", "tensor")
    return jax.shard_map(
        functools.partial(on_device, mesh.shape["dp"] // 2),
        mesh=mesh,
        in_specs=(spec,) * 5,
        out_specs=(spec,) * 5,
        check_vma=False,
    )
```

time: 768 us -> 115 us (0.15)
  blocking collectives: 520 us -> 0 us
  waiting for transfers between devices: 152 us -> 0 us
  Pallas kernels: 0 us -> 108 us
  starting transfers between devices: 65 us -> 0 us
  between operations: 14.8 us -> 0.65 us
  matrix products: 10.5 us -> 0 us
    all_gather x5 -> x0, blocking collectives: 359 us -> none  [the longest x1 159 us: on_device(): lax.all_gather(cotangent, 'dp', axis=0, tiled=True)]
    unnamed x1 -> x0, blocking collectives: 161 us -> none
    reduce_scatter x3 -> x0, waiting for transfers between devices: 149 us -> none  [the longest x1 81 us: on_device(): lax.psum_scatter(gate_part, 'tensor', scatter_dimension=0, tiled=True)]
    pallas_call x0 -> x1, Pallas kernels: none -> 108 us  [on_device(): pl.pallas_call(functools.partial(kernel, zs), out_shape=(block, block, gr...]
    unnamed x16 -> x0, starting transfers between devices: 64.9 us -> none
    dot_general x9 -> x0, matrix products: 10.5 us -> none  [the longest x3 4.57 us: contract_first(): lax.dot_general(left, right, (((0,), (0,)), ((), ())), preferred_element_...]
  transfers between devices with their start and end apart: 19 -> 0, of which waited for: 3 -> 0; matrix products, arithmetic and copies ran while one was open for 1% -> 0% of each run, Pallas kernels for 0% -> 0%
where the time goes in v1:
time: 115 us; the launch traced here: 114 us
  Pallas kernels  108 us (94%)
  local copies, waits for them, and re-layouts  5.81 us (5%)
    pallas_call x1, Pallas kernels, on_device(): pl.pallas_call(functools.partial(kernel, zs), out_shape=(block, block, gr...  108 us
    unnamed x13, local copies, waits for them, and re-layouts  5.81 us

profile of v1, /device:TPU:6, one launch (start us, length us, event | category | flops | bytes accessed | tf_op | source)
XLA Modules:
  0.0 114.1 jit_solution(14213324957520498773)
XLA Ops:
  0.6 107.7 %ffn.1 = (bf16[6,512]{1,0:T(8,128)(2,1)}, bf16[6,512]{1,0:T(8,128)(2,1)}, bf16[448,512]{1,0:T(8,128)(2,1)}, bf16[448,512]{1,0:T(8,128)(2,1)}, bf16[448,512]{1,0:T(8,128)(2,1)}) custom-call(bf16[6,512]{1,0:T(8,128)(2,1)} %act_ref.1, bf16[6,512]{1,0:T(8,128)(2,1)} %cot_ref.1, bf16[448,512]{1,0:T(8,128)(2,1)} %wg_hbm.1, bf16[448,512]{1,0:T(8,128)(2,1)} %wu_hbm.1, ...), custom_call_target="tpu_custom_call" | custom-call | flops 1585446912 | bytes 2752512 | tf_op jit(solution)/shard_map/ffn/pallas_call | solution.py:363
  108.3 0.0 copy-start.3
  108.3 0.7 copy-done.3
  109.0 0.0 copy-start.2
  109.0 0.6 copy.19
  109.6 0.1 copy-done.2
  109.7 0.6 copy.20
  110.3 0.0 copy-start.1
  110.3 1.9 %copy.21 = bf16[448,512]{1,0:T(8,128)(2,1)} copy(bf16[448,512]{1,0:T(8,128)(2,1)} %get-tuple-element.12) | data formatting | bytes 917504
  112.2 0.0 copy-done.1
  112.2 0.0 copy-start
  112.2 0.8 copy.22
  113.0 0.4 copy-done
  113.4 0.8 copy.23
Async XLA Ops:
  108.3 0.7 copy-start.3
  109.0 0.7 copy-start.2
  110.3 1.9 %copy-start.1 = (bf16[448,512]{1,0:T(8,128)(2,1)S(1)}, bf16[448,512]{1,0:T(8,128)(2,1)}, u32[]{:S(2)}) copy-start(bf16[448,512]{1,0:T(8,128)(2,1)} %get-tuple-element.13) | copy-start | bytes 1376260
  112.2 1.2 %copy-start = (bf16[448,512]{1,0:T(8,128)(2,1)S(1)}, bf16[448,512]{1,0:T(8,128)(2,1)}, u32[]{:S(2)}) copy-start(bf16[448,512]{1,0:T(8,128)(2,1)} %get-tuple-element.14) | copy-start | bytes 1376260

commit v2 on v1

--- a/solution.py
+++ b/solution.py
@@ -12,12 +12,16 @@
 F32 = jnp.float32
 BF16 = jnp.bfloat16
 
-NEAR = (0, 1, -1, 2, -2, 3, -3, 4)
-FAR = (0, 8, -8, 16)
+NEAR = (0, 1, -1, 2)
+FAR = (0, 4, -4, 8, -8, 12, -12, 16)
+F0, P4, M4, P8, M8, P12, M12, F16 = range(8)
+ABOVE = (F0, P4, P8, P12)
+BELOW = {M4: F0, M8: M4, M12: M8, F16: M12}
 TOK = 6
 QUARTERS = 4
 ROWS = 2 * TOK * QUARTERS
-GROUP = TOK * len(NEAR)
+BLOCKS = 8
+GROUP = TOK * BLOCKS
 N_COPIES = 160
 
 
@@ -54,7 +58,7 @@
     out_ref, gin_ref, gg_ref, gu_ref, gd_ref,
     wg, wu, wd, unfold, back, stage16, g_buf, acts, cots,
     pa, pb, ra, rb, qa, qb, a1, b1, sa, sb, a2, b2, ha, hb, hd,
-    own_sum, xs, xr_buf, rbuf, rw, rw7a, rw7b, fsend, frecv,
+    own_sum, xs, xr_buf, rbuf, rw, fsend, frecv,
     local_sem, send_sem, recv_sem,
 ):
     dp, tn = lax.axis_index("dp"), lax.axis_index("tensor")
@@ -84,7 +88,7 @@
         loads.append(cp)
 
     barrier = pltpu.get_barrier_semaphore()
-    peers = [z_dev(d) for d in (8, -8, 4, -4, 3, -3, 2, -2, 1, -1)]
+    peers = [z_dev(d) for d in (8, -8, 4, -4, 2, -2, 1, -1)]
     peers += [x2_dev, x1_dev, c_dev] + [t_dev(xl, y_at(d), c) for d in (1, 2, 3)]
     for peer in peers:
         pl.semaphore_signal(barrier, inc=1, device_id=peer, device_id_type=MESH)
@@ -112,55 +116,73 @@
 
     pl.semaphore_wait(barrier, len(peers))
 
+    own = g_buf.at[0, F0, 0]
     far = {}
-    far[2] = send(g_buf.at[0, 0, 0], g_buf.at[0, 2, 0], z_dev(8))
-    far[1] = send(g_buf.at[0, 0, 0], g_buf.at[0, 1, 0], z_dev(-8))
-    near = {}
+    far[M8] = send(own, g_buf.at[0, M8, 0], z_dev(8))
+    far[P8] = send(own, g_buf.at[0, P8, 0], z_dev(-8))
+    far[M4] = send(own, g_buf.at[0, M4, 0], z_dev(4))
+    far[P4] = send(own, g_buf.at[0, P4, 0], z_dev(-4))
+    near, across = {}, {}
 
     def spread(f):
-        for w in range(1, 7):
-            near[f, w] = send(g_buf.at[0, f, 0], g_buf.at[0, f, w], z_dev(-NEAR[w]))
-        if f in (0, 1):
-            near[f, 7] = send(g_buf.at[0, f, 0], g_buf.at[0, f, 7], z_dev(-4))
-        if f in (0, 2):
-            near[2 if f == 0 else 3, 7] = send(
-                g_buf.at[0, f, 0], g_buf.at[0, 2 if f == 0 else 3, 7], z_dev(4)
-            )
-
-    across = {}
+        block = g_buf.at[0, f, 0]
+        near[f, 1] = send(block, g_buf.at[0, f, 1], z_dev(-1))
+        near[f, 2] = send(block, g_buf.at[0, f, 2], z_dev(1))
+        if f in ABOVE:
+            near[f, 3] = send(block, g_buf.at[0, f, 3], z_dev(-2))
+        for slot, source in BELOW.items():
+            if source == f:
+                near[slot, 3] = send(block, g_buf.at[0, slot, 3], z_dev(2))
 
     def cross(f):
-        for w in range(1, 8):
+        for w in (1, 2, 3):
             near[f, w].wait_recv()
         across[f] = send(g_buf.at[0, f], g_buf.at[1, f], x2_dev)
 
-    def order(x, f):
-        blocks = g_buf[x, f].reshape(8 * ROWS, 128)
+    def order(x, g):
+        blocks = g_buf[x, 2 * g : 2 * g + 2].reshape(BLOCKS * ROWS, 128)
         for q in range(QUARTERS):
             rows = dot(unfold[q], blocks).astype(BF16)
             lanes = slice(q * 128, (q + 1) * 128)
-            acts[x, f, :, lanes] = rows[:GROUP]
-            cots[x, f, :, lanes] = rows[GROUP:]
-
-    spread(0)
-    far[2].wait_recv()
-    far[3] = send(g_buf.at[0, 2, 0], g_buf.at[0, 3, 0], z_dev(8))
-    spread(2)
-    far[1].wait_recv()
-    spread(1)
+            acts[x, g, :, lanes] = rows[:GROUP]
+            cots[x, g, :, lanes] = rows[GROUP:]
+
+    def order_other(g):
+        across[2 * g].wait_recv()
+        across[2 * g + 1].wait_recv()
+        order(1, g)
+
+    spread(F0)
+    far[P4].wait_recv()
+    spread(P4)
+    far[M4].wait_recv()
+    spread(M4)
+    far[M8].wait_recv()
+    far[F16] = send(g_buf.at[0, M8, 0], g_buf.at[0, F16, 0], z_dev(8))
+    far[M12] = send(g_buf.at[0, M8, 0], g_buf.at[0, M12, 0], z_dev(4))
+    far[P8].wait_recv()
+    far[P12] = send(g_buf.at[0, P8, 0], g_buf.at[0, P12, 0], z_dev(-4))
+    spread(P8)
+    spread(M8)
+    cross(F0)
+    cross(P4)
+    cross(M4)
     for cp in loads:
         cp.wait()
-    cross(0)
     order(0, 0)
-    far[3].wait_recv()
-    spread(3)
-    cross(1)
-    cross(2)
+    cross(P8)
+    cross(M8)
+    far[M12].wait_recv()
+    spread(M12)
+    far[P12].wait_recv()
+    spread(P12)
     order(0, 1)
+    far[F16].wait_recv()
+    spread(F16)
+    cross(P12)
+    cross(M12)
     order(0, 2)
-    across[0].wait_recv()
-    order(1, 0)
-    cross(3)
+    cross(F16)
     order(0, 3)
 
     pair = {}
@@ -183,9 +205,8 @@
         pair[x, 1] = send(pb.at[co, x], rb.at[x], c_dev)
 
     partial_sums(0)
-    for f in (1, 2, 3):
-        across[f].wait_recv()
-        order(1, f)
+    for g in range(4):
+        order_other(g)
     partial_sums(1)
 
     pair[0, 1].wait_recv()
@@ -249,56 +270,72 @@
         h, dg, du = [hd[j, x].reshape(4 * GROUP, 512)[:, :448] for j in range(3)]
         return dot(h, wd[...]), dot(dg, wg[...]) + dot(du, wu[...])
 
-    f_order = (3, 2, 1, 0)
+    over = {}
+
+    def give(g):
+        over[g] = send(xs.at[g], xr_buf.at[g], x2_dev)
+
     fwd, bwd = hidden_sums(1)
-    over = {}
-    for f in f_order:
-        r = slice(f * GROUP, (f + 1) * GROUP)
-        xs[f, 0:GROUP] = fwd[r].astype(BF16)
-        xs[f, GROUP : 2 * GROUP] = bwd[r].astype(BF16)
-        over[f] = send(xs.at[f], xr_buf.at[f], x2_dev)
+    for g in range(4):
+        r = slice(g * GROUP, (g + 1) * GROUP)
+        xs[g, 0:GROUP] = fwd[r].astype(BF16)
+        xs[g, GROUP : 2 * GROUP] = bwd[r].astype(BF16)
+    give(3)
+    give(2)
     fwd, bwd = hidden_sums(0)
-    for f in f_order:
-        r = slice(f * GROUP, (f + 1) * GROUP)
-        own_sum[f, 0:GROUP] = fwd[r]
-        own_sum[f, GROUP : 2 * GROUP] = bwd[r]
-
-    step3, step0 = {}, {}
-    for f in f_order:
-        over[f].wait_recv()
-        both = (own_sum[f] + xr_buf[f].astype(F32)).astype(BF16)
-        rows = jnp.zeros((8 * ROWS, 128), F32)
+    give(1)
+    give(0)
+    for g in range(4):
+        r = slice(g * GROUP, (g + 1) * GROUP)
+        own_sum[g, 0:GROUP] = fwd[r]
+        own_sum[g, GROUP : 2 * GROUP] = bwd[r]
+
+    part_in = {}
+
+    def collect(g):
+        over[g].wait_recv()
+        both = (own_sum[g] + xr_buf[g].astype(F32)).astype(BF16)
+        rows = jnp.zeros((BLOCKS * ROWS, 128), F32)
         for q in range(QUARTERS):
             rows += dot(back[q], both[:, q * 128 : (q + 1) * 128])
         rows = rows.astype(BF16)
-        for w in range(8):
-            rbuf[w, f] = rows[w * ROWS : (w + 1) * ROWS]
-        if f == 3:
-            for w in range(1, 7):
-                step3[w] = send(rbuf.at[w, 3], rw.at[w, 3], z_dev(NEAR[w]))
-        if f == 2:
-            minus4 = send(rbuf.at[7, pl.ds(2, 2)], rw7b, z_dev(-4))
-    for w in range(1, 7):
-        step0[w] = send(rbuf.at[w, pl.ds(0, 3)], rw.at[w, pl.ds(0, 3)], z_dev(NEAR[w]))
-    plus4 = send(rbuf.at[7, pl.ds(0, 2)], rw7a, z_dev(4))
+        for i in range(BLOCKS):
+            rbuf[2 * g + i // 4, i % 4] = rows[i * ROWS : (i + 1) * ROWS]
+        for f in (2 * g + 1, 2 * g):
+            part_in[f, 0] = send(rbuf.at[f, 1], rw.at[f, 0], z_dev(1))
+            part_in[f, 1] = send(rbuf.at[f, 2], rw.at[f, 1], z_dev(-1))
+            if f in ABOVE:
+                part_in[f, 2] = send(rbuf.at[f, 3], rw.at[f, 2], z_dev(2))
+            else:
+                part_in[BELOW[f], 3] = send(rbuf.at[f, 3], rw.at[BELOW[f], 3], z_dev(-2))
 
     def near_sum(f):
-        total = rbuf[0, f].astype(F32)
-        for w in range(1, 7):
-            total += rw[w, f].astype(F32)
+        total = rbuf[f, 0].astype(F32)
+        for i in range(4):
+            if (f, i) in part_in:
+                part_in[f, i].wait_recv()
+                total += rw[f, i].astype(F32)
         return total
 
-    for w in range(1, 7):
-        step3[w].wait_recv()
-    fsend[0] = near_sum(3).astype(BF16)
-    far16 = send(fsend.at[0], frecv.at[0], z_dev(8))
-
-    for w in range(1, 7):
-        step0[w].wait_recv()
-    minus4.wait_recv()
-    plus4.wait_recv()
-    fsend[1] = (near_sum(2) + rw7b[1].astype(F32)).astype(BF16)
-    back8 = send(fsend.at[1], frecv.at[1], z_dev(-8))
+    onward = {}
+
+    def pass_on(i, f, dev, *others):
+        total = near_sum(f)
+        for o in others:
+            onward[o].wait_recv()
+            total += frecv[o].astype(F32)
+        fsend[i] = total.astype(BF16)
+        onward[i] = send(fsend.at[i], frecv.at[i], dev)
+
+    collect(3)
+    collect(2)
+    pass_on(0, F16, z_dev(8))
+    collect(1)
+    pass_on(2, M12, z_dev(-4))
+    pass_on(1, P12, z_dev(4))
+    collect(0)
+    pass_on(5, P4, z_dev(4))
+    pass_on(6, M4, z_dev(-4))
 
     a_all = acts[...].reshape(8 * GROUP, 512)
     c_all = cots[...].reshape(8 * GROUP, 512)
@@ -309,23 +346,31 @@
         ref[256:448] = t_dot(d[:, 256:448], rows).astype(BF16)
 
     weight_grad(1, a_all, gg_ref)
+    pass_on(4, M8, z_dev(-8), 2)
+    pass_on(3, P8, z_dev(8), 1, 0)
     weight_grad(2, a_all, gu_ref)
-    far16.wait_recv()
-    fsend[2] = (near_sum(1) + rw7a[1].astype(F32) + frecv[0].astype(F32)).astype(BF16)
-    on8 = send(fsend.at[2], frecv.at[2], z_dev(8))
     weight_grad(0, c_all, gd_ref)
 
-    total = near_sum(0) + rw7a[0].astype(F32) + rw7b[0].astype(F32)
-    back8.wait_recv()
-    total += frecv[1].astype(F32)
-    on8.wait_recv()
-    total = (total + frecv[2].astype(F32)).astype(BF16)
+    total = near_sum(F0)
+    for o in (5, 6, 4, 3):
+        onward[o].wait_recv()
+        total += frecv[o].astype(F32)
+    total = total.astype(BF16)
     for q in range(QUARTERS):
         stage16[:, q * 128 : (q + 1) * 128] = dot(last_ref[q], total)
     out_ref[...] = stage16[0:TOK].astype(BF16)
     gin_ref[...] = stage16[8 : 8 + TOK].astype(BF16)
     for cp in sent:
         cp.wait_send()
+
+
+def hand_over(*refs):
+    sem = refs[-1]
+    copies = [pltpu.make_async_copy(refs[i], refs[5 + i], sem.at[i]) for i in range(5)]
+    for cp in copies:
+        cp.start()
+    for cp in copies:
+        cp.wait()
 
 
 def on_device(zs, activations, cotangent, w_gate, w_up, w_down):
@@ -340,7 +385,7 @@
         pltpu.VMEM(weight, BF16), pltpu.VMEM(weight, BF16), pltpu.VMEM(weight, BF16),
         pltpu.VMEM(unfold.shape, BF16), pltpu.VMEM(back.shape, BF16),
         pltpu.VMEM((16, features), F32),
-        pltpu.VMEM((2, 4, 8, ROWS, 128), BF16),
+        pltpu.VMEM((2, 8, 4, ROWS, 128), BF16),
         pltpu.VMEM((2, 4, GROUP, features), BF16), pltpu.VMEM((2, 4, GROUP, features), BF16),
         pltpu.VMEM((2, 4, 2, row3, 128), F32), pltpu.VMEM((2, 2, 4, row3, 128), F32),
         pltpu.VMEM((4, 2, row3, 128), F32), pltpu.VMEM((2, 4, row3, 128), F32),
@@ -353,14 +398,13 @@
         pltpu.VMEM((4, 2 * GROUP, features), F32),
         pltpu.VMEM((4, 2 * GROUP, features), BF16), pltpu.VMEM((4, 2 * GROUP, features), BF16),
         pltpu.VMEM((8, 4, ROWS, 128), BF16), pltpu.VMEM((8, 4, ROWS, 128), BF16),
-        pltpu.VMEM((2, ROWS, 128), BF16), pltpu.VMEM((2, ROWS, 128), BF16),
-        pltpu.VMEM((3, ROWS, 128), BF16), pltpu.VMEM((3, ROWS, 128), BF16),
+        pltpu.VMEM((7, ROWS, 128), BF16), pltpu.VMEM((7, ROWS, 128), BF16),
         pltpu.SemaphoreType.DMA((5,)),
         pltpu.SemaphoreType.DMA((N_COPIES,)), pltpu.SemaphoreType.DMA((N_COPIES,)),
     ]
     block = jax.ShapeDtypeStruct((tokens, features), BF16)
     grad = jax.ShapeDtypeStruct(weight, BF16)
-    return pl.pallas_call(
+    results = pl.pallas_call(
         functools.partial(kernel, zs),
         out_shape=(block, block, grad, grad, grad),
         in_specs=[vmem, vmem, anywhere, anywhere, anywhere, vmem, anywhere, anywhere, vmem],
@@ -375,6 +419,14 @@
         ),
         name="ffn",
     )(activations, cotangent, w_gate, w_up, w_down, fold, unfold, back, last)
+    return pl.pallas_call(
+        hand_over,
+        out_shape=(block, block, grad, grad, grad),
+        in_specs=[vmem] * 5,
+        out_specs=(anywhere,) * 5,
+        scratch_shapes=[pltpu.SemaphoreType.DMA((5,))],
+        name="hand_over",
+    )(*results)
 
 
 def solution(mesh):

time: 115 us -> 104 us (0.904)
  Pallas kernels: 108 us -> 101 us
  local copies, waits for them, and re-layouts: 5.81 us -> 0 us
    pallas_call x1, Pallas kernels: 108 us -> 99 us  [on_device(): pl.pallas_call(functools.partial(kernel, zs), out_shape=(block, block, gr...]
    unnamed x13 -> x0, local copies, waits for them, and re-layouts: 5.81 us -> none
    pallas_call x0 -> x1, Pallas kernels: none -> 2.45 us  [on_device(): pl.pallas_call(hand_over, out_shape=(block, block, grad, grad, grad), in_...]
where the time goes in v2:
time: 104 us; the launch traced here: 102 us
  Pallas kernels  101 us (97%)
    pallas_call x1, Pallas kernels, on_device(): pl.pallas_call(functools.partial(kernel, zs), out_shape=(block, block, gr...  99 us
    pallas_call x1, Pallas kernels, on_device(): pl.pallas_call(hand_over, out_shape=(block, block, grad, grad, grad), in_...  2.45 us

profile of v2, /device:TPU:6, one launch (start us, length us, event | category | flops | bytes accessed | tf_op | source)
XLA Modules:
  0.0 102.1 jit_solution(2475221775785245933)
XLA Ops:
  0.6 99.0 %ffn.1 = (bf16[6,512]{1,0:T(8,128)(2,1)}, bf16[6,512]{1,0:T(8,128)(2,1)}, bf16[448,512]{1,0:T(8,128)(2,1)}, bf16[448,512]{1,0:T(8,128)(2,1)}, bf16[448,512]{1,0:T(8,128)(2,1)}) custom-call(bf16[6,512]{1,0:T(8,128)(2,1)} %act_ref.1, bf16[6,512]{1,0:T(8,128)(2,1)} %cot_ref.1, bf16[448,512]{1,0:T(8,128)(2,1)} %wg_hbm.1, bf16[448,512]{1,0:T(8,128)(2,1)} %wu_hbm.1, ...), custom_call_target="tpu_custom_call" | custom-call | flops 1585446912 | bytes 2752512 | tf_op jit(solution)/shard_map/ffn/pallas_call | solution.py:407
  99.6 2.4 %hand_over.1 = (bf16[6,512]{1,0:T(8,128)(2,1)}, bf16[6,512]{1,0:T(8,128)(2,1)}, bf16[448,512]{1,0:T(8,128)(2,1)}, bf16[448,512]{1,0:T(8,128)(2,1)}, bf16[448,512]{1,0:T(8,128)(2,1)}) custom-call(bf16[6,512]{1,0:T(8,128)(2,1)} %get-tuple-element.10.refs_0_, bf16[6,512]{1,0:T(8,128)(2,1)} %get-tuple-element.11.refs_1_, ...), custom_call_target="tpu_custom_call" | custom-call | tf_op jit(solution)/shard_map/hand_over/pallas_call | solution.py:422

commit v3 on v2

--- a/solution.py
+++ b/solution.py
@@ -75,7 +75,10 @@
     def y_at(d):
         return (y + d) % 4
 
-    x2_dev = (z * 2 + (1 - xh), tn)
+    def x2_at(d):
+        return (((z + (d + zs)) % zs) * 2 + (1 - xh), tn)
+
+    x2_dev = x2_at(0)
     x1_dev = t_dev(xo, y, c)
     c_dev = t_dev(xl, y, co)
 
@@ -89,7 +92,7 @@
 
     barrier = pltpu.get_barrier_semaphore()
     peers = [z_dev(d) for d in (8, -8, 4, -4, 2, -2, 1, -1)]
-    peers += [x2_dev, x1_dev, c_dev] + [t_dev(xl, y_at(d), c) for d in (1, 2, 3)]
+    peers += [x2_dev, x2_at(1), x2_at(-1), x1_dev, c_dev] + [t_dev(xl, y_at(d), c) for d in (1, 2, 3)]
     for peer in peers:
         pl.semaphore_signal(barrier, inc=1, device_id=peer, device_id_type=MESH)
 
@@ -149,7 +152,11 @@
 
     def order_other(g):
         across[2 * g].wait_recv()
-        across[2 * g + 1].wait_recv()
+        if g == 3:
+            for cp in last:
+                cp.wait_recv()
+        else:
+            across[2 * g + 1].wait_recv()
         order(1, g)
 
     spread(F0)
@@ -158,9 +165,10 @@
     far[M4].wait_recv()
     spread(M4)
     far[M8].wait_recv()
-    far[F16] = send(g_buf.at[0, M8, 0], g_buf.at[0, F16, 0], z_dev(8))
+    far[P8].wait_recv()
+    odd = z % 2
+    far[F16] = send(g_buf.at[0, M8 - odd, 0], g_buf.at[0, F16, 0], z_dev(8 + (zs - 16) * odd))
     far[M12] = send(g_buf.at[0, M8, 0], g_buf.at[0, M12, 0], z_dev(4))
-    far[P8].wait_recv()
     far[P12] = send(g_buf.at[0, P8, 0], g_buf.at[0, P12, 0], z_dev(-4))
     spread(P8)
     spread(M8)
@@ -179,10 +187,19 @@
     order(0, 1)
     far[F16].wait_recv()
     spread(F16)
+    last = [
+        send(g_buf.at[0, F16, 0], g_buf.at[1, F16, 0], x2_dev),
+        send(g_buf.at[0, F16, 0], g_buf.at[1, F16, 1], x2_at(-1)),
+        send(g_buf.at[0, F16, 0], g_buf.at[1, F16, 2], x2_at(1)),
+    ]
     cross(P12)
     cross(M12)
+    near[F16, 3].wait_recv()
+    last.append(send(g_buf.at[0, F16, 3], g_buf.at[1, F16, 3], x2_dev))
     order(0, 2)
-    cross(F16)
+    order_other(0)
+    near[F16, 1].wait_recv()
+    near[F16, 2].wait_recv()
     order(0, 3)
 
     pair = {}
@@ -204,26 +221,43 @@
         pair[x, 0] = send(pa.at[co, :, x], ra.at[:, x], c_dev)
         pair[x, 1] = send(pb.at[co, x], rb.at[x], c_dev)
 
+    first_a = []
+
+    def along_y(x):
+        pair[x, 0].wait_recv()
+        qa[:, x] = pa[c, :, x] + ra[:, x]
+        for d in (2, 1, 3):
+            dev = t_dev(xl, y_at(d), c)
+            first_a.append(send(qa.at[y_at(d), x], a1.at[d - 1, x], dev))
+
     partial_sums(0)
-    for g in range(4):
-        order_other(g)
+    order_other(1)
+    along_y(0)
+    order_other(2)
+    order_other(3)
     partial_sums(1)
 
     pair[0, 1].wait_recv()
     pair[1, 1].wait_recv()
-    qb[...] = pb[c] + rb[...]
-    first_b = send(qb.at[xo], b1, x1_dev)
-    pair[0, 0].wait_recv()
-    pair[1, 0].wait_recv()
-    qa[...] = pa[c] + ra[...]
-    first_a = [send(qa.at[y_at(d)], a1.at[d - 1], t_dev(xl, y_at(d), c)) for d in (2, 1, 3)]
-    first_b.wait_recv()
-    sb[...] = qb[xl] + b1[...]
-    second_b = [send(sb.at[y_at(d)], b2.at[d - 1], t_dev(xl, y_at(d), c)) for d in (2, 1, 3)]
+    first_b, second_b = {}, []
+    for d in (2, 1, 3, 0):
+        r = y_at(d)
+        qb[xo, r] = pb[c, xo, r] + rb[xo, r]
+        first_b[d] = send(qb.at[xo, r], b1.at[r], x1_dev)
+    along_y(1)
+    qb[xl] = pb[c, xl] + rb[xl]
+    for d in (2, 1, 3):
+        r = y_at(d)
+        first_b[d].wait_recv()
+        sb[r] = qb[xl, r] + b1[r]
+        second_b.append(send(sb.at[r], b2.at[d - 1], t_dev(xl, r, c)))
     for cp in first_a:
         cp.wait_recv()
-    sa[...] = qa[y] + a1[0] + a1[1] + a1[2]
+    sa[xo] = qa[y, xo] + a1[0, xo] + a1[1, xo] + a1[2, xo]
     second_a = send(sa.at[xo], a2, x1_dev)
+    sa[xl] = qa[y, xl] + a1[0, xl] + a1[1, xl] + a1[2, xl]
+    first_b[0].wait_recv()
+    sb[y] = qb[xl, y] + b1[y]
 
     def finish(sums):
         gate, up, grad = sums[0:GROUP], sums[GROUP : 2 * GROUP], sums[2 * GROUP : 3 * GROUP]
@@ -281,10 +315,8 @@
         xs[g, 0:GROUP] = fwd[r].astype(BF16)
         xs[g, GROUP : 2 * GROUP] = bwd[r].astype(BF16)
     give(3)
+    fwd, bwd = hidden_sums(0)
     give(2)
-    fwd, bwd = hidden_sums(0)
-    give(1)
-    give(0)
     for g in range(4):
         r = slice(g * GROUP, (g + 1) * GROUP)
         own_sum[g, 0:GROUP] = fwd[r]
@@ -327,29 +359,28 @@
         fsend[i] = total.astype(BF16)
         onward[i] = send(fsend.at[i], frecv.at[i], dev)
 
+    def weight_grad(j, tokens, ref):
+        d = hd[j].reshape(8 * GROUP, 512)
+        rows = tokens[...].reshape(8 * GROUP, 512)
+        ref[0:256] = t_dot(d[:, 0:256], rows).astype(BF16)
+        ref[256:448] = t_dot(d[:, 256:448], rows).astype(BF16)
+
+    weight_grad(1, acts, gg_ref)
     collect(3)
+    give(1)
+    give(0)
     collect(2)
     pass_on(0, F16, z_dev(8))
     collect(1)
     pass_on(2, M12, z_dev(-4))
     pass_on(1, P12, z_dev(4))
+    weight_grad(2, acts, gu_ref)
     collect(0)
+    pass_on(4, M8, z_dev(-8), 2)
+    pass_on(3, P8, z_dev(8), 1, 0)
     pass_on(5, P4, z_dev(4))
     pass_on(6, M4, z_dev(-4))
-
-    a_all = acts[...].reshape(8 * GROUP, 512)
-    c_all = cots[...].reshape(8 * GROUP, 512)
-
-    def weight_grad(j, rows, ref):
-        d = hd[j].reshape(8 * GROUP, 512)
-        ref[0:256] = t_dot(d[:, 0:256], rows).astype(BF16)
-        ref[256:448] = t_dot(d[:, 256:448], rows).astype(BF16)
-
-    weight_grad(1, a_all, gg_ref)
-    pass_on(4, M8, z_dev(-8), 2)
-    pass_on(3, P8, z_dev(8), 1, 0)
-    weight_grad(2, a_all, gu_ref)
-    weight_grad(0, c_all, gd_ref)
+    weight_grad(0, cots, gd_ref)
 
     total = near_sum(F0)
     for o in (5, 6, 4, 3):

time: 104 us -> 102 us (0.981); the launches traced: 102 us -> 101 us
  no operation moved by 1% of the time
where the time goes in v3:
time: 102 us; the launch traced here: 101 us
  Pallas kernels  101 us (99%)
    pallas_call x1, Pallas kernels, on_device(): pl.pallas_call(functools.partial(kernel, zs), out_shape=(block, block, gr...  98.2 us
    pallas_call x1, Pallas kernels, on_device(): pl.pallas_call(hand_over, out_shape=(block, block, grad, grad, grad), in_...  2.45 us

profile of v3, /device:TPU:6, one launch (start us, length us, event | category | flops | bytes accessed | tf_op | source)
XLA Modules:
  0.0 101.3 jit_solution(17875500201960683479)
XLA Ops:
  0.6 98.2 %ffn.1 = (bf16[6,512]{1,0:T(8,128)(2,1)}, bf16[6,512]{1,0:T(8,128)(2,1)}, bf16[448,512]{1,0:T(8,128)(2,1)}, bf16[448,512]{1,0:T(8,128)(2,1)}, bf16[448,512]{1,0:T(8,128)(2,1)}) custom-call(bf16[6,512]{1,0:T(8,128)(2,1)} %act_ref.1, bf16[6,512]{1,0:T(8,128)(2,1)} %cot_ref.1, bf16[448,512]{1,0:T(8,128)(2,1)} %wg_hbm.1, bf16[448,512]{1,0:T(8,128)(2,1)} %wu_hbm.1, ...), custom_call_target="tpu_custom_call" | custom-call | flops 1585446912 | bytes 2752512 | tf_op jit(solution)/shard_map/ffn/pallas_call | solution.py:438
  98.8 2.4 %hand_over.1 = (bf16[6,512]{1,0:T(8,128)(2,1)}, bf16[6,512]{1,0:T(8,128)(2,1)}, bf16[448,512]{1,0:T(8,128)(2,1)}, bf16[448,512]{1,0:T(8,128)(2,1)}, bf16[448,512]{1,0:T(8,128)(2,1)}) custom-call(bf16[6,512]{1,0:T(8,128)(2,1)} %get-tuple-element.10.refs_0_, bf16[6,512]{1,0:T(8,128)(2,1)} %get-tuple-element.11.refs_1_, ...), custom_call_target="tpu_custom_call" | custom-call | tf_op jit(solution)/shard_map/hand_over/pallas_call | solution.py:453

commit v4 on v3

--- a/solution.py
+++ b/solution.py
@@ -54,8 +54,9 @@
 
 
 def kernel(
-    zs, act_ref, cot_ref, wg_hbm, wu_hbm, wd_hbm, fold_ref, unfold_hbm, back_hbm, last_ref,
-    out_ref, gin_ref, gg_ref, gu_ref, gd_ref,
+    zs, act_hbm, cot_hbm, wg_hbm, wu_hbm, wd_hbm, fold_hbm, unfold_hbm, back_hbm, last_hbm,
+    out_ref, gin_ref, gg_hbm, gu_hbm, gd_hbm,
+    act_ref, cot_ref, fold_ref, last_ref, grads,
     wg, wu, wd, unfold, back, stage16, g_buf, acts, cots,
     pa, pb, ra, rb, qa, qb, a1, b1, sa, sb, a2, b2, ha, hb, hd,
     own_sum, xs, xr_buf, rbuf, rw, fsend, frecv,
@@ -82,19 +83,20 @@
     x1_dev = t_dev(xo, y, c)
     c_dev = t_dev(xl, y, co)
 
-    loads = []
-    for i, (s, d) in enumerate(
-        ((wg_hbm, wg), (wu_hbm, wu), (wd_hbm, wd), (unfold_hbm, unfold), (back_hbm, back))
-    ):
-        cp = pltpu.make_async_copy(s, d, local_sem.at[i])
-        cp.start()
-        loads.append(cp)
-
     barrier = pltpu.get_barrier_semaphore()
     peers = [z_dev(d) for d in (8, -8, 4, -4, 2, -2, 1, -1)]
     peers += [x2_dev, x2_at(1), x2_at(-1), x1_dev, c_dev] + [t_dev(xl, y_at(d), c) for d in (1, 2, 3)]
     for peer in peers:
         pl.semaphore_signal(barrier, inc=1, device_id=peer, device_id_type=MESH)
+
+    loads = []
+    for i, (s, d) in enumerate(
+        ((act_hbm, act_ref), (cot_hbm, cot_ref), (fold_hbm, fold_ref), (wg_hbm, wg), (wu_hbm, wu), (wd_hbm, wd),
+         (unfold_hbm, unfold), (back_hbm, back), (last_hbm, last_ref))
+    ):
+        cp = pltpu.make_async_copy(s, d, local_sem.at[i])
+        cp.start()
+        loads.append(cp)
 
     sent = []
 
@@ -109,6 +111,8 @@
         return cp
 
     stage16[...] = jnp.zeros_like(stage16)
+    for cp in loads[:3]:
+        cp.wait()
     stage16[0:TOK] = act_ref[...].astype(F32)
     stage16[8 : 8 + TOK] = cot_ref[...].astype(F32)
     raw = stage16[...].astype(BF16)
@@ -175,7 +179,7 @@
     cross(F0)
     cross(P4)
     cross(M4)
-    for cp in loads:
+    for cp in loads[3:]:
         cp.wait()
     order(0, 0)
     cross(P8)
@@ -359,13 +363,18 @@
         fsend[i] = total.astype(BF16)
         onward[i] = send(fsend.at[i], frecv.at[i], dev)
 
-    def weight_grad(j, tokens, ref):
+    stores = []
+
+    def weight_grad(j, tokens, result):
+        ref = grads.at[j]
         d = hd[j].reshape(8 * GROUP, 512)
         rows = tokens[...].reshape(8 * GROUP, 512)
         ref[0:256] = t_dot(d[:, 0:256], rows).astype(BF16)
         ref[256:448] = t_dot(d[:, 256:448], rows).astype(BF16)
-
-    weight_grad(1, acts, gg_ref)
+        stores.append(pltpu.make_async_copy(ref, result, local_sem.at[9 + j]))
+        stores[-1].start()
+
+    weight_grad(1, acts, gg_hbm)
     collect(3)
     give(1)
     give(0)
@@ -374,13 +383,13 @@
     collect(1)
     pass_on(2, M12, z_dev(-4))
     pass_on(1, P12, z_dev(4))
-    weight_grad(2, acts, gu_ref)
+    weight_grad(2, acts, gu_hbm)
     collect(0)
     pass_on(4, M8, z_dev(-8), 2)
     pass_on(3, P8, z_dev(8), 1, 0)
     pass_on(5, P4, z_dev(4))
     pass_on(6, M4, z_dev(-4))
-    weight_grad(0, cots, gd_ref)
+    weight_grad(0, cots, gd_hbm)
 
     total = near_sum(F0)
     for o in (5, 6, 4, 3):
@@ -393,15 +402,22 @@
     gin_ref[...] = stage16[8 : 8 + TOK].astype(BF16)
     for cp in sent:
         cp.wait_send()
+    for cp in stores:
+        cp.wait()
 
 
 def hand_over(*refs):
     sem = refs[-1]
-    copies = [pltpu.make_async_copy(refs[i], refs[5 + i], sem.at[i]) for i in range(5)]
-    for cp in copies:
-        cp.start()
-    for cp in copies:
-        cp.wait()
+    loads = [pltpu.make_async_copy(refs[i], refs[10 + i], sem.at[i]) for i in range(5)]
+    stores = [pltpu.make_async_copy(refs[10 + i], refs[5 + i], sem.at[5 + i]) for i in range(5)]
+    turns = (2, 3, 4, 0, 1)
+    for i in turns:
+        loads[i].start()
+    for i in turns:
+        loads[i].wait()
+        stores[i].start()
+    for i in turns:
+        stores[i].wait()
 
 
 def on_device(zs, activations, cotangent, w_gate, w_up, w_down):
@@ -413,6 +429,9 @@
     weight = (hidden, features)
     row3 = 3 * GROUP
     scratch = [
+        pltpu.VMEM((tokens, features), BF16), pltpu.VMEM((tokens, features), BF16),
+        pltpu.VMEM(fold.shape, BF16), pltpu.VMEM(last.shape, BF16),
+        pltpu.VMEM((3,) + weight, BF16),
         pltpu.VMEM(weight, BF16), pltpu.VMEM(weight, BF16), pltpu.VMEM(weight, BF16),
         pltpu.VMEM(unfold.shape, BF16), pltpu.VMEM(back.shape, BF16),
         pltpu.VMEM((16, features), F32),
@@ -430,7 +449,7 @@
         pltpu.VMEM((4, 2 * GROUP, features), BF16), pltpu.VMEM((4, 2 * GROUP, features), BF16),
         pltpu.VMEM((8, 4, ROWS, 128), BF16), pltpu.VMEM((8, 4, ROWS, 128), BF16),
         pltpu.VMEM((7, ROWS, 128), BF16), pltpu.VMEM((7, ROWS, 128), BF16),
-        pltpu.SemaphoreType.DMA((5,)),
+        pltpu.SemaphoreType.DMA((12,)),
         pltpu.SemaphoreType.DMA((N_COPIES,)), pltpu.SemaphoreType.DMA((N_COPIES,)),
     ]
     block = jax.ShapeDtypeStruct((tokens, features), BF16)
@@ -438,8 +457,8 @@
     results = pl.pallas_call(
         functools.partial(kernel, zs),
         out_shape=(block, block, grad, grad, grad),
-        in_specs=[vmem, vmem, anywhere, anywhere, anywhere, vmem, anywhere, anywhere, vmem],
-        out_specs=(vmem,) * 5,
+        in_specs=[anywhere] * 9,
+        out_specs=(vmem,) * 2 + (anywhere,) * 3,
         scratch_shapes=scratch,
         compiler_params=pltpu.CompilerParams(
             collective_id=0, has_side_effects=True, vmem_limit_bytes=56 * 2**20
@@ -453,9 +472,10 @@
     return pl.pallas_call(
         hand_over,
         out_shape=(block, block, grad, grad, grad),
-        in_specs=[vmem] * 5,
+        in_specs=[anywhere] * 5,
         out_specs=(anywhere,) * 5,
-        scratch_shapes=[pltpu.SemaphoreType.DMA((5,))],
+        scratch_shapes=[pltpu.VMEM(v.shape, BF16) for v in results]
+        + [pltpu.SemaphoreType.DMA((10,))],
         name="hand_over",
     )(*results)
 

time: 102 us -> 100 us (0.980)
  Pallas kernels: 101 us -> 99.2 us
    pallas_call x1, Pallas kernels: 98.2 us -> 97 us  [on_device(): pl.pallas_call(functools.partial(kernel, zs), out_shape=(block, block, gr...]
where the time goes in v4:
time: 100 us; the launch traced here: 99.9 us
  Pallas kernels  99.2 us (99%)
    pallas_call x1, Pallas kernels, on_device(): pl.pallas_call(functools.partial(kernel, zs), out_shape=(block, block, gr...  97 us
    pallas_call x1, Pallas kernels, on_device(): pl.pallas_call(hand_over, out_shape=(block, block, grad, grad, grad), in_...  2.18 us

profile of v4, /device:TPU:6, one launch (start us, length us, event | category | flops | bytes accessed | tf_op | source)
XLA Modules:
  0.0 99.9 jit_solution(10376630901591611038)
XLA Ops:
  0.6 97.0 %ffn.1 = (bf16[6,512]{1,0:T(8,128)(2,1)}, bf16[6,512]{1,0:T(8,128)(2,1)}, bf16[448,512]{1,0:T(8,128)(2,1)}, bf16[448,512]{1,0:T(8,128)(2,1)}, bf16[448,512]{1,0:T(8,128)(2,1)}) custom-call(bf16[6,512]{1,0:T(8,128)(2,1)} %act_hbm.1, bf16[6,512]{1,0:T(8,128)(2,1)} %cot_hbm.1, bf16[448,512]{1,0:T(8,128)(2,1)} %wg_hbm.1, bf16[448,512]{1,0:T(8,128)(2,1)} %wu_hbm.1, ...), custom_call_target="tpu_custom_call" | custom-call | flops 1585446912 | bytes 2752512 | tf_op jit(solution)/shard_map/ffn/pallas_call | solution.py:457
  97.7 2.2 %hand_over.1 = (bf16[6,512]{1,0:T(8,128)(2,1)}, bf16[6,512]{1,0:T(8,128)(2,1)}, bf16[448,512]{1,0:T(8,128)(2,1)}, bf16[448,512]{1,0:T(8,128)(2,1)}, bf16[448,512]{1,0:T(8,128)(2,1)}) custom-call(bf16[6,512]{1,0:T(8,128)(2,1)} %get-tuple-element.10.refs_0_, bf16[6,512]{1,0:T(8,128)(2,1)} %get-tuple-element.11.refs_1_, ...), custom_call_target="tpu_custom_call" | custom-call | tf_op jit(solution)/shard_map/hand_over/pallas_call | solution.py:472

commit v5 on v4

--- a/solution.py
+++ b/solution.py
@@ -293,16 +293,20 @@
         cores.append(send(ha.at[c, y_at(4 - d)], ha.at[c, y_at(4 - d)], c_dev))
     wide_b.wait_recv()
     cores.append(send(hb.at[c, xo], hb.at[c, xo], c_dev))
+    def lay_out(half):
+        low = pl.ds(pl.multiple_of(half * 256, 128), 128)
+        high = pl.ds(pl.multiple_of(half * 256 + 128, 128), 128)
+        for j in range(3):
+            part = slice(j * GROUP, (j + 1) * GROUP)
+            for x in range(2):
+                for f in range(4):
+                    hd[j, x, f, :, low] = ha[half, f, x, part]
+                    hd[j, x, f, :, high] = hb[half, x, f, part]
+
+    lay_out(c)
     for cp in cores:
         cp.wait_recv()
-
-    for j in range(3):
-        part = slice(j * GROUP, (j + 1) * GROUP)
-        for half in range(2):
-            for x in range(2):
-                for f in range(4):
-                    hd[j, x, f, :, half * 256 : half * 256 + 128] = ha[half, f, x, part]
-                    hd[j, x, f, :, half * 256 + 128 : half * 256 + 256] = hb[half, x, f, part]
+    lay_out(co)
 
     def hidden_sums(x):
         h, dg, du = [hd[j, x].reshape(4 * GROUP, 512)[:, :448] for j in range(3)]

time: 100 us -> 99.3 us (level)
  Pallas kernels: 99.2 us -> 98.1 us
    pallas_call x1, Pallas kernels: 97 us -> 95.9 us  [on_device(): pl.pallas_call(functools.partial(kernel, zs), out_shape=(block, block, gr...]
where the time goes in v5:
time: 99.3 us; the launch traced here: 98.7 us
  Pallas kernels  98.1 us (99%)
    pallas_call x1, Pallas kernels, on_device(): pl.pallas_call(functools.partial(kernel, zs), out_shape=(block, block, gr...  95.9 us
    pallas_call x1, Pallas kernels, on_device(): pl.pallas_call(hand_over, out_shape=(block, block, grad, grad, grad), in_...  2.18 us

profile of v5, /device:TPU:6, one launch (start us, length us, event | category | flops | bytes accessed | tf_op | source)
XLA Modules:
  0.0 98.7 jit_solution(11613508809049380772)
XLA Ops:
  0.6 95.9 %ffn.1 = (bf16[6,512]{1,0:T(8,128)(2,1)}, bf16[6,512]{1,0:T(8,128)(2,1)}, bf16[448,512]{1,0:T(8,128)(2,1)}, bf16[448,512]{1,0:T(8,128)(2,1)}, bf16[448,512]{1,0:T(8,128)(2,1)}) custom-call(bf16[6,512]{1,0:T(8,128)(2,1)} %act_hbm.1, bf16[6,512]{1,0:T(8,128)(2,1)} %cot_hbm.1, bf16[448,512]{1,0:T(8,128)(2,1)} %wg_hbm.1, bf16[448,512]{1,0:T(8,128)(2,1)} %wu_hbm.1, ...), custom_call_target="tpu_custom_call" | custom-call | flops 1585446912 | bytes 2752512 | tf_op jit(solution)/shard_map/ffn/pallas_call | solution.py:461
  96.5 2.2 %hand_over.1 = (bf16[6,512]{1,0:T(8,128)(2,1)}, bf16[6,512]{1,0:T(8,128)(2,1)}, bf16[448,512]{1,0:T(8,128)(2,1)}, bf16[448,512]{1,0:T(8,128)(2,1)}, bf16[448,512]{1,0:T(8,128)(2,1)}) custom-call(bf16[6,512]{1,0:T(8,128)(2,1)} %get-tuple-element.10.refs_0_, bf16[6,512]{1,0:T(8,128)(2,1)} %get-tuple-element.11.refs_1_, ...), custom_call_target="tpu_custom_call" | custom-call | tf_op jit(solution)/shard_map/hand_over/pallas_call | solution.py:476
